TPU v7x, 256 devices: a whole 4x4x8 slice. The times are simulated.
256 devices in a mesh: row: 16 (over x, y_hi, core), col: 16 (over y_lo, z).
Axes of the slice: x: 4, y: 4 (y_hi: 2, y_lo: 2; y = y_hi * 2 + y_lo), z: 8, core: 2. Of those that a mesh axis runs over, the one named last changes fastest.
Arguments:
- latents: bfloat16 [2048, 6144], P('col', 'row'), may hold values from -6 to 6
- w_in: bfloat16 [6144, 24576], P('row', 'col'), may hold values from -0.078125 to 0.078125
- w_out: bfloat16 [24576, 6144], P('col', 'row'), may hold values from -0.0390625 to 0.0390625
- cotangent: bfloat16 [2048, 6144], P('col', 'row'), may hold values from -0.3125 to 0.3125
Outputs:
- mixed: bfloat16 [2048, 6144], P('col', 'row')
- grad_w_in: bfloat16 [6144, 24576], P('row', 'col')
- grad_w_out: bfloat16 [24576, 6144], P('col', 'row')
All inputs are finite; a program needn't handle non-finite values.
Results may differ from a plain program's by a relative error of at most 0.03.
Values may be sent and summed in bfloat16 or wider, within the bound.
A program may use at most 128 MiB of HBM per device.

v0:
```python
import jax
import jax.numpy as jnp
from jax import lax
from jax.sharding import PartitionSpec as P


def gelu_parts(hidden):
    cdf = 0.5 * (1.0 + jax.scipy.special.erf(hidden * 0.7071067811865476))
    pdf = jnp.exp(-0.5 * hidden * hidden) * 0.3989422804014327
    return (hidden * cdf, cdf + hidden * pdf)


def per_device(latents, w_in, w_out, cotangent):
    tokens_all = lax.all_gather(latents, "col", axis=0, tiled=True)
    block = tokens_all
    hidden = lax.psum_scatter(
        jnp.dot(block, w_in, preferred_element_type=jnp.float32).astype(jnp.bfloat16),
        "row",
        scatter_dimension=0,
        tiled=True,
    ).astype(jnp.float32)
    act, slope = gelu_parts(hidden)
    act = act.astype(jnp.bfloat16)
    act_all = lax.all_gather(act, "row", axis=0, tiled=True)
    block = act_all
    mixed = lax.psum_scatter(
        jnp.dot(block, w_out, preferred_element_type=jnp.float32).astype(jnp.bfloat16),
        "col",
        scatter_dimension=0,
        tiled=True,
    )
    cot_all = lax.all_gather(cotangent, "col", axis=0, tiled=True)
    block = cot_all
    grad_act = lax.psum_scatter(
        lax.dot_general(
            block, w_out, (((1,), (1,)), ((), ())), preferred_element_type=jnp.float32
        ).astype(jnp.bfloat16),
        "row",
        scatter_dimension=0,
        tiled=True,
    ).astype(jnp.float32)
    grad_hidden = (grad_act * slope).astype(jnp.bfloat16)
    grad_w_out = lax.dot_general(
        act_all, cot_all, (((0,), (0,)), ((), ())), preferred_element_type=jnp.float32
    )
    block = tokens_all
    grad_w_in = lax.dot_general(
        block,
        lax.all_gather(grad_hidden, "row", axis=0, tiled=True),
        (((0,), (0,)), ((), ())),
        preferred_element_type=jnp.float32,
    )
    return (mixed, grad_w_in.astype(jnp.bfloat16), grad_w_out.astype(jnp.bfloat16))


def solution(mesh):
    placed = (P("col", "row"), P("row", "col"), P("col", "row"), P("col", "row"))
    return jax.shard_map(
        per_device,
        mesh=mesh,
        in_specs=placed,
        out_specs=(P("col", "row"), P("row", "col"), P("col", "row")),
        check_vma=False,
    )
```

profile of v0, /device:TPU:1, one launch (start us, length us, event | category | flops | bytes accessed | tf_op | source)
XLA Modules:
  0.0 565.0 jit_solution(925925690740267204)
XLA Ops:
  7.2 0.0 copy-start
  7.2 0.0 all-gather.9.cloned.1.call-start
  7.2 0.7 all-gather.9.cloned.1.call-update
  7.9 0.0 all-gather.5.cloned.1.call-start
  8.0 0.7 all-gather.5.cloned.1.call-update
  8.7 0.0 reduce-scatter.8.cloned.1.call-start
  8.7 65.8 %all-gather.9.cloned.1.call-done = bf16[2048,384]{1,0:T(8,128)(2,1)} async-done(((bf16[128,384]{1,0:T(8,128)(2,1)}), bf16[2048,384]{1,0:T(8,128)(2,1)}) %all-gather.9.cloned.1.call-update) | async-done | bytes 1572880 | tf_op jit(solution)/shard_map/all_gather | solution.py:32
  74.5 0.0 copy-done
  74.5 6.8 %convolution_convert_fusion = bf16[2048,1536]{1,0:T(8,128)(2,1)} fusion(bf16[2048,384]{1,0:T(8,128)(2,1)} %all-gather.9.cloned.1.call-done, bf16[1536,384]{1,0:T(8,128)(2,1)S(1)} %copy-done), kind=kOutput, calls=%fused_computation | convolution fusion | flops 2419064832 | bytes 9043968 | tf_op jit(solution)/shard_map/dot_general | solution.py:35
  81.3 0.0 copy-start.1
  81.3 0.0 reduce-scatter.8.cloned.1.call-update
  81.3 0.0 reduce-scatter.4.cloned.1.call-start
  81.4 62.5 %all-gather.5.cloned.1.call-done = bf16[2048,384]{1,0:T(8,128)(2,1)} async-done(((bf16[128,384]{1,0:T(8,128)(2,1)}), bf16[2048,384]{1,0:T(8,128)(2,1)}) %all-gather.5.cloned.1.call-update) | async-done | bytes 1572880 | tf_op jit(solution)/shard_map/all_gather | solution.py:14
  143.9 0.0 copy-done.1
  143.9 6.7 %convolution_convert_fusion.1 = bf16[2048,1536]{1,0:T(8,128)(2,1)} fusion(bf16[2048,384]{1,0:T(8,128)(2,1)} %all-gather.5.cloned.1.call-done, bf16[384,1536]{1,0:T(8,128)(2,1)S(1)} %copy-done.1), kind=kOutput, calls=%fused_computation.1 | convolution fusion | flops 2419064832 | bytes 9043968 | tf_op jit(solution)/shard_map/dot_general | solution.py:17
  150.6 0.0 reduce-scatter.4.cloned.1.call-update
  150.6 0.0 all-gather.7.cloned.1.call-start
  150.7 100.5 %reduce-scatter.8.cloned.1.call-done = bf16[128,1536]{1,0:T(8,128)(2,1)} async-done(((bf16[2048,1536]{1,0:T(8,128)(2,1)}), bf16[128,1536]{1,0:T(8,128)(2,1)}) %reduce-scatter.8.cloned.1.call-update) | async-done | bytes 393232 | tf_op jit(solution)/shard_map/reduce_scatter | solution.py:34
  251.1 100.5 %reduce-scatter.4.cloned.1.call-done = bf16[128,1536]{1,0:T(8,128)(2,1)} async-done(((bf16[2048,1536]{1,0:T(8,128)(2,1)}), bf16[128,1536]{1,0:T(8,128)(2,1)}) %reduce-scatter.4.cloned.1.call-update) | async-done | bytes 393232 | tf_op jit(solution)/shard_map/reduce_scatter | solution.py:16
  351.6 2.4 fusion.9
  354.0 0.0 all-gather.7.cloned.1.call-update
  354.0 0.0 all-gather.11.cloned.1.call-start
  354.1 0.5 all-gather.11.cloned.1.call-update
  354.6 0.2 reduce-scatter.6.cloned.1.call-start
  354.8 69.8 %all-gather.7.cloned.1.call-done = bf16[2048,1536]{1,0:T(8,128)(2,1)} async-done(((bf16[128,1536]{1,0:T(8,128)(2,1)}), bf16[2048,1536]{1,0:T(8,128)(2,1)}) %all-gather.7.cloned.1.call-update) | async-done | bytes 6291472 | tf_op jit(solution)/shard_map/all_gather | solution.py:24
  424.6 7.4 %convolution_convert_fusion.4 = bf16[2048,384]{1,0:T(8,128)(2,1)} fusion(bf16[2048,1536]{1,0:T(8,128)(2,1)} %all-gather.7.cloned.1.call-done, bf16[1536,384]{1,0:T(8,128)(2,1)S(1)} %copy-done), kind=kOutput, calls=%fused_computation.4 | convolution fusion | flops 2416705536 | bytes 9043968 | tf_op jit(solution)/shard_map/dot_general | solution.py:27
  431.9 0.0 reduce-scatter.6.cloned.1.call-update
  432.0 63.5 %all-gather.11.cloned.1.call-done = bf16[2048,1536]{1,0:T(8,128)(2,1)} async-done(((bf16[128,1536]{1,0:T(8,128)(2,1)}), bf16[2048,1536]{1,0:T(8,128)(2,1)}) %all-gather.11.cloned.1.call-update) | async-done | bytes 6291472 | tf_op jit(solution)/shard_map/all_gather | solution.py:49
  495.5 6.7 %fusion = bf16[384,1536]{0,1:T(8,128)(2,1)S(1)} fusion(bf16[2048,1536]{1,0:T(8,128)(2,1)} %all-gather.11.cloned.1.call-done, bf16[2048,384]{1,0:T(8,128)(2,1)} %all-gather.5.cloned.1.call-done), kind=kOutput, calls=%fused_computation.5 | convolution fusion | flops 2416508928 | bytes 9043968 | tf_op jit(solution)/shard_map/dot_general | solution.py:47
  502.2 1.5 copy.7
  503.6 7.7 %convolution_convert_fusion.2 = bf16[1536,384]{1,0:T(8,128)(2,1)} fusion(bf16[2048,1536]{1,0:T(8,128)(2,1)} %all-gather.7.cloned.1.call-done, bf16[2048,384]{1,0:T(8,128)(2,1)} %all-gather.9.cloned.1.call-done), kind=kOutput, calls=%fused_computation.2 | convolution fusion | flops 2416508928 | bytes 9043968 | tf_op jit(solution)/shard_map/dot_general | solution.py:43
  511.3 46.8 %reduce-scatter.6.cloned.1.call-done = bf16[128,384]{1,0:T(8,128)(2,1)} async-done(((bf16[2048,384]{1,0:T(8,128)(2,1)}), bf16[128,384]{1,0:T(8,128)(2,1)}) %reduce-scatter.6.cloned.1.call-update) | async-done | bytes 98320 | tf_op jit(solution)/shard_map/reduce_scatter | solution.py:26
Async XLA Ops:
  7.2 67.3 %copy-start = (bf16[1536,384]{1,0:T(8,128)(2,1)S(1)}, bf16[1536,384]{1,0:T(8,128)(2,1)}, u32[]{:S(2)}) copy-start(bf16[1536,384]{1,0:T(8,128)(2,1)} %param.6) | copy-start | bytes 3538948
  7.2 67.3 %all-gather.9.cloned.1.call-start = ((), (), s32[]{:S(2)}) async-start(), calls=%async_computation.7 | async-start | bytes 1671168 | tf_op jit(solution)/shard_map/all_gather | solution.py:32
  7.9 136.0 %all-gather.5.cloned.1.call-start = ((), (), s32[]{:S(2)}) async-start(), calls=%async_computation.3 | async-start | bytes 1671168 | tf_op jit(solution)/shard_map/all_gather | solution.py:14
  8.7 242.5 %reduce-scatter.8.cloned.1.call-start = ((), (), s32[]{:S(2)}) async-start(), calls=%async_computation.8 | async-start | bytes 6684672 | tf_op jit(solution)/shard_map/reduce_scatter | solution.py:34
  81.3 62.6 %copy-start.1 = (bf16[384,1536]{1,0:T(8,128)(2,1)S(1)}, bf16[384,1536]{1,0:T(8,128)(2,1)}, u32[]{:S(2)}) copy-start(bf16[384,1536]{1,0:T(8,128)(2,1)} %param.5) | copy-start | bytes 3538948
  81.3 270.2 %reduce-scatter.4.cloned.1.call-start = ((), (), s32[]{:S(2)}) async-start(), calls=%async_computation.4 | async-start | bytes 6684672 | tf_op jit(solution)/shard_map/reduce_scatter | solution.py:16
  150.6 274.0 %all-gather.7.cloned.1.call-start = ((), (), s32[]{:S(2)}) async-start(), calls=%async_computation.5 | async-start | bytes 6684672 | tf_op jit(solution)/shard_map/all_gather | solution.py:24
  354.0 141.5 %all-gather.11.cloned.1.call-start = ((), (), s32[]{:S(2)}) async-start(), calls=%async_computation.9 | async-start | bytes 6684672 | tf_op jit(solution)/shard_map/all_gather | solution.py:49
  354.6 203.5 %reduce-scatter.6.cloned.1.call-start = ((), (), s32[]{:S(2)}) async-start(), calls=%async_computation.6 | async-start | bytes 1671168 | tf_op jit(solution)/shard_map/reduce_scatter | solution.py:26
Sparse Core Ops, SparseCore 0:
  9.8 64.6 all-gather.8
  76.3 67.5 all-gather.4
  148.3 102.7 reduce-scatter.7
  255.4 96.1 reduce-scatter.3
  354.7 69.8 all-gather.6
  427.7 67.7 all-gather.10
  498.6 59.4 reduce-scatter.5
where the time goes:
time: 576 us; the launch traced here: 565 us
  waiting for transfers between devices  511 us (89%)
  matrix products  35.3 us (6%)
  between operations  14.1 us (2%)
    reduce_scatter x1, waiting for transfers between devices, per_device(): lax.psum_scatter(jnp.dot(block, w_in, preferred_element_type=jnp.float32)...  100 us
    reduce_scatter x1, waiting for transfers between devices, per_device(): lax.psum_scatter(lax.dot_general(block, w_out, (((1,), (1,)), ((), ())),...  100 us
    all_gather x1, waiting for transfers between devices, per_device(): act_all = lax.all_gather(act, 'row', axis=0, tiled=True)  69.8 us
    all_gather x1, waiting for transfers between devices, per_device(): cot_all = lax.all_gather(cotangent, 'col', axis=0, tiled=True)  65.8 us
    all_gather x1, waiting for transfers between devices, per_device(): lax.all_gather(grad_hidden, 'row', axis=0, tiled=True)  63.5 us
    all_gather x1, waiting for transfers between devices, per_device(): tokens_all = lax.all_gather(latents, 'col', axis=0, tiled=True)  62.5 us
    reduce_scatter x1, waiting for transfers between devices, per_device(): lax.psum_scatter(jnp.dot(block, w_out, preferred_element_type=jnp.float32...  46.8 us
  transfers between devices with their start and end apart: 7, of which 7 were waited for; matrix products, arithmetic and copies ran while one was open for 7% of the time, Pallas kernels for 0%

commit v1 on v0

v1 whole, which is shorter than its diff:
```python
import jax
import jax.numpy as jnp
from jax import lax
from jax.experimental import pallas as pl
from jax.experimental.pallas import tpu as pltpu
from jax.sharding import PartitionSpec as P

MESH = pl.DeviceIdType.MESH
BF = jnp.bfloat16
F32 = jnp.float32

TOK, FEAT, HID = 128, 384, 1536
ROWS, WIDE = 256, 768
CH = 8
PIECE, HALF = 64, 32

NN = (((1,), (0,)), ((), ()))
NT = (((1,), (1,)), ((), ()))
TN = (((0,), (0,)), ((), ()))


def dot(a, b, dims):
    return lax.dot_general(a, b, dims, preferred_element_type=F32)


def kernel(
    lat, w_in, w_out, cot,
    mixed, g_in, g_out,
    X, WI, WO, PT, FAR, CMB, RX, YS, YR, HS, SL, A, MO, MS, MR, MT, MIX, OUT, GW, GB,
    s_loc, s_w, s_ws, s_x, s_xs, s_c, s_cs, s_far, s_rx, s_yr, s_ya, s_ag, s_fw,
    s_snd, s_mr, s_ms, s_mix, s_mixs, s_g, s_gs, s_gl,
):
    row, col = lax.axis_index("row"), lax.axis_index("col")
    x, yh, core = row // 4, (row // 2) % 2, row % 2
    yl, z = col // 8, col % 8

    def dev(x=x, yh=yh, core=core, yl=yl, z=z):
        return ((x * 2 + yh) * 2 + core, yl * 8 + z)

    right, left, across = (x + 1) % 4, (x + 3) % 4, (x + 2) % 4
    east, west = dev(x=right), dev(x=left)
    twin = dev(core=1 - core)
    pair = dev(yh=1 - yh)
    beside = dev(yl=1 - yl)
    up, down = dev(z=(z + 1) % 8), dev(z=(z + 7) % 8)

    barrier = pltpu.get_barrier_semaphore()
    for peer in (east, west, twin, pair):
        pl.semaphore_signal(barrier, inc=1, device_id=peer, device_id_type=MESH)
    for step in range(1, 16):
        pl.semaphore_signal(
            barrier, inc=1, device_id=(row, (col + step) % 16), device_id_type=MESH
        )

    def send(src, dst, send_sem, recv_sem, to):
        pltpu.make_async_remote_copy(
            src_ref=src, dst_ref=dst, send_sem=send_sem, recv_sem=recv_sem,
            device_id=to, device_id_type=MESH,
        ).start()

    def wait(ref, sem):
        pltpu.make_async_copy(ref, ref, sem).wait()

    def ds(start, size):
        return pl.ds(pl.multiple_of(start, size), size)

    mine = ds(core * WIDE, WIDE)
    other = ds((1 - core) * WIDE, WIDE)
    own, far = pl.ds(0, FEAT), pl.ds(FEAT, FEAT)
    s0, s1 = pl.ds(0, TOK), pl.ds(TOK, TOK)

    local = [
        pltpu.make_async_copy(lat, X.at[0, s0, own], s_loc.at[0]),
        pltpu.make_async_copy(w_in.at[:, mine], WI.at[own], s_loc.at[1]),
        pltpu.make_async_copy(w_out.at[mine], WO.at[:, own], s_loc.at[2]),
        pltpu.make_async_copy(cot, X.at[8, s0, own], s_loc.at[3]),
    ]
    for c in local:
        c.start()

    pl.semaphore_wait(barrier, 19)

    def first(src, j):
        send(src, X.at[j, s0, far], s_cs.at[j], s_c.at[j], twin)
        send(src, X.at[j, s1, own], s_xs.at[j], s_x.at[j], beside)
        send(src, X.at[j + 1, s0, own], s_xs.at[j], s_x.at[j + 1], up)
        send(src, X.at[j + 2, s0, own], s_xs.at[j], s_x.at[j + 2], down)

    def second(j):
        block = X.at[j, s1, own]
        wait(block, s_x.at[j])
        send(block, X.at[j + 1, s1, own], s_xs.at[j], s_x.at[j + 1], up)
        send(block, X.at[j + 2, s1, own], s_xs.at[j], s_x.at[j + 2], down)
        send(block, X.at[j, s1, far], s_cs.at[j], s_c.at[j], twin)

    first(lat, 0)
    send(w_in.at[:, other], WI.at[far], s_ws.at[0], s_w.at[0], twin)
    send(w_out.at[other], WO.at[:, far], s_ws.at[1], s_w.at[1], twin)
    second(0)
    for c in local:
        c.wait()
    wait(WI.at[own], s_w.at[0])
    wait(WO.at[:, own], s_w.at[1])

    def gather(j):
        k = j % CH
        whole = X.at[j, :, own]
        wait(whole, s_x.at[j])
        send(whole, X.at[j, :, far], s_cs.at[j], s_c.at[j], twin)
        onward = dev(z=(z + 1 + (1 - k % 2) * 6) % 8)

        @pl.when(k <= 4)
        def _():
            send(whole, X.at[j + 2, :, own], s_xs.at[j], s_x.at[j + 2], onward)

        @pl.when(k == 5)
        def _():
            send(X.at[j, s0, own], X.at[j + 2, s0, own], s_xs.at[j], s_x.at[j + 2], onward)

        @pl.when(k == 6)
        def _():
            send(X.at[j, s1, own], X.at[j + 1, s1, own], s_xs.at[j], s_x.at[j + 1], onward)

    def part(j):
        wait(X.at[j, :, own], s_c.at[j])

        @pl.when(j < CH)
        def _():
            PT[j] = dot(X[j], WI[...], NN).astype(BF)

        @pl.when(j >= CH)
        def _():
            PT[j] = dot(X[j], WO[...], NT).astype(BF)

        ss = s_snd.at[j]
        send(PT.at[j, ds(across * PIECE, HALF)], FAR.at[j, 0], ss, s_far.at[j], east)
        send(PT.at[j, ds(across * PIECE + HALF, HALF)], FAR.at[j, 1], ss, s_far.at[j], west)
        send(PT.at[j, ds(right * PIECE + HALF, HALF)], RX.at[j, 0, pl.ds(HALF, HALF)], ss, s_rx.at[j], east)
        send(PT.at[j, ds(left * PIECE, HALF)], RX.at[j, 1, pl.ds(0, HALF)], ss, s_rx.at[j], west)

    def combine(j):
        wait(FAR.at[j], s_far.at[j])
        ss = s_snd.at[j]
        a = PT[j, ds(right * PIECE, HALF), :].astype(F32) + FAR[j, 0].astype(F32)
        CMB[j, 0] = a.astype(BF)
        b = PT[j, ds(left * PIECE + HALF, HALF), :].astype(F32) + FAR[j, 1].astype(F32)
        CMB[j, 1] = b.astype(BF)
        send(CMB.at[j, 0], RX.at[j, 0, pl.ds(0, HALF)], ss, s_rx.at[j], east)
        send(CMB.at[j, 1], RX.at[j, 1, pl.ds(HALF, HALF)], ss, s_rx.at[j], west)

    def total(j):
        wait(RX.at[j], s_rx.at[j])

        def summed(which):
            t = PT[j, ds(x * PIECE + which * HALF, HALF), :].astype(F32)
            t = t + RX[j, 0, ds(which * HALF, HALF), :].astype(F32)
            return t + RX[j, 1, ds(which * HALF, HALF), :].astype(F32)

        YS[j] = summed(1 - yh).astype(BF)
        send(YS.at[j], YR.at[j], s_snd.at[j], s_yr.at[j], pair)
        HS[j] = summed(yh)

    def point(j):
        wait(YR.at[j], s_yr.at[j])
        h = HS[j] + YR[j].astype(F32)
        here = ds(x * PIECE + yh * HALF, HALF)

        @pl.when(j < CH)
        def _():
            cdf = 0.5 * (1.0 + lax.erf(h * 0.7071067811865476))
            pdf = jnp.exp(-0.5 * h * h) * 0.3989422804014327
            A[j, here, :] = (h * cdf).astype(BF)
            SL[j] = cdf + h * pdf

        @pl.when(j >= CH)
        def _():
            A[j, here, :] = (h * SL[j - CH]).astype(BF)

        block = A.at[j, here]
        send(block, block, s_snd.at[j], s_ya.at[j], pair)

    def spread(j):
        wait(YR.at[j], s_ya.at[j])
        block = A.at[j, ds(x * PIECE, PIECE)]
        send(block, block, s_snd.at[j], s_ag.at[j], east)
        send(block, block, s_snd.at[j], s_ag.at[j], west)

    def onward(j):
        wait(RX.at[j], s_ag.at[j])
        a = A.at[j, ds(left * PIECE, HALF)]
        b = A.at[j, ds(right * PIECE + HALF, HALF)]
        send(a, a, s_snd.at[j], s_fw.at[j], east)
        send(b, b, s_snd.at[j], s_fw.at[j], west)

    def use(j):
        wait(FAR.at[j], s_fw.at[j])

        @pl.when(j < CH)
        def _():
            m = dot(A[j], WO[...], NN)
            MS[j] = m[:, FEAT:].astype(BF)
            send(MS.at[j], MR.at[j], s_ms.at[j], s_mr.at[j], twin)
            MO[j] = m[:, :FEAT]

        @pl.when(j >= CH)
        def _():
            GW[1] = GW[1] + dot(X[j - CH], A[j], TN)

    def use_late(j):
        GW[0] = GW[0] + dot(A[j], X[j + CH], TN)

        @pl.when(j == CH - 1)
        def _():
            GB[0] = GW[0].astype(BF)
            pltpu.make_async_copy(GB.at[0, :, own], g_out.at[mine], s_gl.at[0]).start()
            send(GB.at[0, :, far], g_out.at[mine], s_gs.at[0], s_g.at[0], twin)

    def mix(j):
        wait(MS.at[j], s_mr.at[j])
        MT[j] = (MO[j] + MR[j].astype(F32)).astype(BF)
        there = (z + j // 2 + 8 - (j % 2) * j) % 8

        @pl.when(j > 0)
        def _():
            send(MT.at[j, s0], MIX.at[2 * j - 1], s_mixs.at[j], s_mix, dev(z=there))

        send(MT.at[j, s1], MIX.at[2 * j], s_mixs.at[j], s_mix, dev(yl=1 - yl, z=there))

    GW[...] = jnp.zeros_like(GW)

    def stage(f, j, lo=0, hi=16):
        @pl.when((j >= lo) & (j < hi))
        def _():
            f(j)

    def step(i, carry):
        stage(combine, i - 2)
        stage(total, i - 3)
        stage(point, i - 4)
        stage(spread, i - 5)
        stage(onward, i - 6)

        @pl.when((i > 0) & (i < 16) & (i != CH))
        def _():
            gather(i)

        stage(part, i - 1)
        stage(mix, i - 8, 0, CH)
        stage(use, i - 7)
        stage(use_late, i - 9, 0, CH)

        @pl.when(i == 2)
        def _():
            first(cot, CH)

        @pl.when(i == 4)
        def _():
            second(CH)

        return carry

    lax.fori_loop(0, 23, step, 0)

    GB[1] = GW[1].astype(BF)
    send(GB.at[1, far], g_in.at[:, mine], s_gs.at[1], s_g.at[1], twin)
    last = pltpu.make_async_copy(GB.at[1, own], g_in.at[:, mine], s_gl.at[1])
    last.start()

    wait(MIX, s_mix)
    t = MT[0, :TOK, :].astype(F32)
    for k in range(15):
        t = t + MIX[k].astype(F32)
    OUT[...] = t.astype(BF)
    done = pltpu.make_async_copy(OUT, mixed, s_gl.at[2])
    done.start()

    wait(WI.at[own], s_ws.at[0])
    wait(WO.at[:, own], s_ws.at[1])

    def drain(j, carry):
        k = j % CH
        wait(A.at[pl.ds(0, 7), pl.ds(0, PIECE)], s_snd.at[j])
        wait(X.at[j, :, own], s_cs.at[j])

        @pl.when(k == 0)
        def _():
            wait(MIX.at[pl.ds(0, 5)], s_xs.at[j])

        @pl.when((k > 0) & (k <= 4))
        def _():
            wait(X.at[j, :, own], s_xs.at[j])

        @pl.when((k == 5) | (k == 6))
        def _():
            wait(X.at[j, s0, own], s_xs.at[j])

        @pl.when(j < CH)
        def _():
            wait(MS.at[j], s_ms.at[j])

        @pl.when((j < CH) & (j > 0))
        def _():
            wait(MT.at[j], s_mixs.at[j])

        @pl.when(j == 0)
        def _():
            wait(MT.at[j, s1], s_mixs.at[j])

        return carry

    lax.fori_loop(0, 16, drain, 0)
    for i, (ref, half) in enumerate(((g_out.at[mine], GB.at[0, :, own]), (g_in.at[:, mine], GB.at[1, own]))):
        wait(half, s_gs.at[i])
        wait(half, s_g.at[i])
        wait(half, s_gl.at[i])
    done.wait()


def per_device(latents, w_in, w_out, cotangent):
    anyspec = pl.BlockSpec(memory_space=pl.ANY)
    V, D = pltpu.VMEM, pltpu.SemaphoreType.DMA
    return pl.pallas_call(
        kernel,
        out_shape=(
            jax.ShapeDtypeStruct((TOK, FEAT), BF),
            jax.ShapeDtypeStruct((FEAT, HID), BF),
            jax.ShapeDtypeStruct((HID, FEAT), BF),
        ),
        in_specs=[anyspec] * 4,
        out_specs=[anyspec] * 3,
        scratch_shapes=[
            V((16, ROWS, WIDE), BF),
            V((WIDE, WIDE), BF),
            V((WIDE, WIDE), BF),
            V((16, ROWS, WIDE), BF),
            V((16, 2, HALF, WIDE), BF),
            V((16, 2, HALF, WIDE), BF),
            V((16, 2, PIECE, WIDE), BF),
            V((16, HALF, WIDE), BF),
            V((16, HALF, WIDE), BF),
            V((16, HALF, WIDE), F32),
            V((CH, HALF, WIDE), F32),
            V((16, ROWS, WIDE), BF),
            V((CH, ROWS, FEAT), F32),
            V((CH, ROWS, FEAT), BF),
            V((CH, ROWS, FEAT), BF),
            V((CH, ROWS, FEAT), BF),
            V((15, TOK, FEAT), BF),
            V((TOK, FEAT), BF),
            V((2, WIDE, WIDE), F32),
            V((2, WIDE, WIDE), BF),
            D((4,)),
            D((2,)),
            D((2,)),
            D((16,)),
            D((16,)),
            D((16,)),
            D((16,)),
            D((16,)),
            D((16,)),
            D((16,)),
            D((16,)),
            D((16,)),
            D((16,)),
            D((16,)),
            D((CH,)),
            D((CH,)),
            D,
            D((CH,)),
            D((2,)),
            D((2,)),
            D((3,)),
        ],
        compiler_params=pltpu.CompilerParams(
            collective_id=0, has_side_effects=True, vmem_limit_bytes=62 * 1024 * 1024
        ),
        cost_estimate=pl.CostEstimate(
            flops=12 * 10**9, bytes_accessed=5 * 10**6, transcendentals=10**6
        ),
    )(latents, w_in, w_out, cotangent)


def solution(mesh):
    placed = (P("col", "row"), P("row", "col"), P("col", "row"), P("col", "row"))
    return jax.shard_map(
        per_device,
        mesh=mesh,
        in_specs=placed,
        out_specs=(P("col", "row"), P("row", "col"), P("col", "row")),
        check_vma=False,
    )
```

time: 576 us -> 160 us (0.28); the launches traced: 565 us -> 157 us
  waiting for transfers between devices: 511 us -> 0 us
  Pallas kernels: 0 us -> 151 us
  matrix products: 35.3 us -> 0 us
  between operations: 14.1 us -> 0.64 us
    all_gather x4 -> x0, waiting for transfers between devices: 262 us -> none  [the longest x1 69.8 us: per_device(): act_all = lax.all_gather(act, 'row', axis=0, tiled=True)]
    reduce_scatter x3 -> x0, waiting for transfers between devices: 248 us -> none  [the longest x1 100 us: per_device(): lax.psum_scatter(jnp.dot(block, w_in, preferred_element_type=jnp.float32)...]
    pallas_call x0 -> x1, Pallas kernels: none -> 151 us  [per_device(): pl.pallas_call(kernel, out_shape=(jax.ShapeDtypeStruct((TOK, FEAT), BF),...]
    dot_general x5 -> x0, matrix products: 35.3 us -> none  [the longest x1 7.7 us: per_device(): lax.dot_general(act_all, cot_all, (((0,), (0,)), ((), ())), preferred_ele...]
  transfers between devices with their start and end apart: 7 -> 0, of which waited for: 7 -> 0; matrix products, arithmetic and copies ran while one was open for 7% -> 0% of each run, Pallas kernels for 0% -> 0%
where the time goes in v1:
time: 160 us; the launch traced here: 157 us
  Pallas kernels  151 us (94%)
  local copies, waits for them, and re-layouts  5.02 us (3%)
    pallas_call x1, Pallas kernels, per_device(): pl.pallas_call(kernel, out_shape=(jax.ShapeDtypeStruct((TOK, FEAT), BF),...  151 us
    unnamed x5, local copies, waits for them, and re-layouts  5.02 us

profile of v1, /device:TPU:1, one launch (start us, length us, event | category | flops | bytes accessed | tf_op | source)
XLA Modules:
  0.0 157.0 jit_solution(15097722628131148027)
XLA Ops:
  0.6 151.4 %shard_map.67 = (bf16[128,384]{1,0:T(8,128)(2,1)}, bf16[384,1536]{1,0:T(8,128)(2,1)}, bf16[1536,384]{1,0:T(8,128)(2,1)}) custom-call(bf16[128,384]{1,0:T(8,128)(2,1)} %lat.1, bf16[384,1536]{1,0:T(8,128)(2,1)} %w_in.1, bf16[1536,384]{1,0:T(8,128)(2,1)} %w_out.1, bf16[128,384]{1,0:T(8,128)(2,1)} %cot.1), custom_call_target="tpu_custom_call" | custom-call | flops 12000000000 | bytes 5000000 | tf_op jit(solution)/shard_map/pallas_call | solution.py:322
  152.0 1.5 copy.10
  153.6 0.0 copy-start
  153.6 2.5 %copy.11 = bf16[384,1536]{1,0:T(8,128)(2,1)} copy(bf16[384,1536]{1,0:T(8,128)(2,1)} %get-tuple-element.7) | data formatting | bytes 2359296
  156.0 0.0 copy-done
  156.0 1.0 copy.12
Async XLA Ops:
  153.6 2.5 %copy-start = (bf16[1536,384]{1,0:T(8,128)(2,1)S(1)}, bf16[1536,384]{1,0:T(8,128)(2,1)}, u32[]{:S(2)}) copy-start(bf16[1536,384]{1,0:T(8,128)(2,1)} %get-tuple-element.8) | copy-start | bytes 3538948

commit v2 on v1

--- a/solution.py
+++ b/solution.py
@@ -12,6 +12,7 @@
 TOK, FEAT, HID = 128, 384, 1536
 ROWS, WIDE = 256, 768
 CH = 8
+LAG = 2
 PIECE, HALF = 64, 32
 
 NN = (((1,), (0,)), ((), ()))
@@ -84,12 +85,12 @@
         send(src, X.at[j, s0, far], s_cs.at[j], s_c.at[j], twin)
         send(src, X.at[j, s1, own], s_xs.at[j], s_x.at[j], beside)
         send(src, X.at[j + 1, s0, own], s_xs.at[j], s_x.at[j + 1], up)
-        send(src, X.at[j + 2, s0, own], s_xs.at[j], s_x.at[j + 2], down)
+        send(src, X.at[j + 1, s1, own], s_xs.at[j], s_x.at[j + 1], down)
 
     def second(j):
         block = X.at[j, s1, own]
         wait(block, s_x.at[j])
-        send(block, X.at[j + 1, s1, own], s_xs.at[j], s_x.at[j + 1], up)
+        send(block, X.at[j + 2, s0, own], s_xs.at[j], s_x.at[j + 2], up)
         send(block, X.at[j + 2, s1, own], s_xs.at[j], s_x.at[j + 2], down)
         send(block, X.at[j, s1, far], s_cs.at[j], s_c.at[j], twin)
 
@@ -107,19 +108,19 @@
         whole = X.at[j, :, own]
         wait(whole, s_x.at[j])
         send(whole, X.at[j, :, far], s_cs.at[j], s_c.at[j], twin)
-        onward = dev(z=(z + 1 + (1 - k % 2) * 6) % 8)
+        low, high = X.at[j, s0, own], X.at[j, s1, own]
+
+        @pl.when(k <= 5)
+        def _():
+            send(low, X.at[j + 2, s0, own], s_xs.at[j], s_x.at[j + 2], up)
 
         @pl.when(k <= 4)
         def _():
-            send(whole, X.at[j + 2, :, own], s_xs.at[j], s_x.at[j + 2], onward)
-
-        @pl.when(k == 5)
-        def _():
-            send(X.at[j, s0, own], X.at[j + 2, s0, own], s_xs.at[j], s_x.at[j + 2], onward)
+            send(high, X.at[j + 2, s1, own], s_xs.at[j], s_x.at[j + 2], down)
 
         @pl.when(k == 6)
         def _():
-            send(X.at[j, s1, own], X.at[j + 1, s1, own], s_xs.at[j], s_x.at[j + 1], onward)
+            send(high, X.at[j + 1, s1, own], s_xs.at[j], s_x.at[j + 1], down)
 
     def part(j):
         wait(X.at[j, :, own], s_c.at[j])
@@ -201,13 +202,11 @@
             MS[j] = m[:, FEAT:].astype(BF)
             send(MS.at[j], MR.at[j], s_ms.at[j], s_mr.at[j], twin)
             MO[j] = m[:, :FEAT]
+            GW[0] = GW[0] + dot(A[j], X[j + CH], TN)
 
         @pl.when(j >= CH)
         def _():
             GW[1] = GW[1] + dot(X[j - CH], A[j], TN)
-
-    def use_late(j):
-        GW[0] = GW[0] + dot(A[j], X[j + CH], TN)
 
         @pl.when(j == CH - 1)
         def _():
@@ -218,48 +217,79 @@
     def mix(j):
         wait(MS.at[j], s_mr.at[j])
         MT[j] = (MO[j] + MR[j].astype(F32)).astype(BF)
-        there = (z + j // 2 + 8 - (j % 2) * j) % 8
-
-        @pl.when(j > 0)
-        def _():
-            send(MT.at[j, s0], MIX.at[2 * j - 1], s_mixs.at[j], s_mix, dev(z=there))
-
-        send(MT.at[j, s1], MIX.at[2 * j], s_mixs.at[j], s_mix, dev(yl=1 - yl, z=there))
+        m = (j + 1) // 2
+        below, above = (z + 8 - m) % 8, (z + m) % 8
+        low, high = MT.at[j, s0], MT.at[j, s1]
+        sems = s_mixs.at[j], s_mix
+
+        @pl.when((j > 0) & (j < CH - 1))
+        def _():
+            line = (yl + j + 1) % 2
+            send(low, MIX.at[2 * j - 1], *sems, dev(yl=line, z=below))
+            send(high, MIX.at[2 * j], *sems, dev(yl=line, z=above))
+
+        @pl.when(j == CH - 1)
+        def _():
+            send(low, MIX.at[2 * j - 1], *sems, dev(z=above))
+
+        @pl.when((j == 0) | (j == CH - 1))
+        def _():
+            send(high, MIX.at[2 * j], *sems, dev(yl=1 - yl, z=above))
 
     GW[...] = jnp.zeros_like(GW)
 
-    def stage(f, j, lo=0, hi=16):
-        @pl.when((j >= lo) & (j < hi))
-        def _():
-            f(j)
-
-    def step(i, carry):
-        stage(combine, i - 2)
-        stage(total, i - 3)
-        stage(point, i - 4)
-        stage(spread, i - 5)
-        stage(onward, i - 6)
-
-        @pl.when((i > 0) & (i < 16) & (i != CH))
-        def _():
-            gather(i)
-
-        stage(part, i - 1)
-        stage(mix, i - 8, 0, CH)
-        stage(use, i - 7)
-        stage(use_late, i - 9, 0, CH)
-
-        @pl.when(i == 2)
+    def reduce_stage(f, t):
+        @pl.when((t >= 0) & (t < CH))
+        def _():
+            f(t)
+
+        @pl.when((t >= CH) & (t < 3 * CH) & (t % 2 == 0))
+        def _():
+            f(t // 2 + CH // 2)
+
+    def spread_stage(f, t):
+        @pl.when((t > CH) & (t < 3 * CH) & (t % 2 == 1))
+        def _():
+            f((t - CH) // 2)
+
+        @pl.when((t >= 3 * CH) & (t < 4 * CH))
+        def _():
+            f(t - 2 * CH)
+
+    def step(t, carry):
+        spread_stage(onward, t - LAG)
+        spread_stage(spread, t)
+        reduce_stage(point, t - 3 * LAG)
+        reduce_stage(total, t - 2 * LAG)
+        reduce_stage(combine, t - LAG)
+
+        @pl.when((t >= 0) & (t < CH - 1))
+        def _():
+            gather(t + 1)
+
+        @pl.when((t >= CH) & (t < 3 * CH - 2) & (t % 2 == 0))
+        def _():
+            gather(t // 2 + CH // 2 + 1)
+
+        reduce_stage(part, t)
+
+        @pl.when((t - 2 * LAG - 1 > CH) & (t - 2 * LAG - 1 < 3 * CH) & ((t - 2 * LAG - 1) % 2 == 1))
+        def _():
+            mix((t - 2 * LAG - 1 - CH) // 2)
+
+        spread_stage(use, t - 2 * LAG)
+
+        @pl.when(t == 3)
         def _():
             first(cot, CH)
 
-        @pl.when(i == 4)
+        @pl.when(t == 6)
         def _():
             second(CH)
 
         return carry
 
-    lax.fori_loop(0, 23, step, 0)
+    lax.fori_loop(0, 4 * CH + 2 * LAG, step, 0)
 
     GB[1] = GW[1].astype(BF)
     send(GB.at[1, far], g_in.at[:, mine], s_gs.at[1], s_g.at[1], twin)

time: 160 us -> 132 us (0.82); the launches traced: 157 us -> 132 us
  Pallas kernels: 151 us -> 126 us
    pallas_call x1, Pallas kernels: 151 us -> 126 us  [per_device(): pl.pallas_call(kernel, out_shape=(jax.ShapeDtypeStruct((TOK, FEAT), BF),...]
where the time goes in v2:
time: 132 us
  Pallas kernels  126 us (95%)
  local copies, waits for them, and re-layouts  5.02 us (4%)
    pallas_call x1, Pallas kernels, per_device(): pl.pallas_call(kernel, out_shape=(jax.ShapeDtypeStruct((TOK, FEAT), BF),...  126 us
    unnamed x5, local copies, waits for them, and re-layouts  5.02 us

profile of v2, /device:TPU:1, one launch (start us, length us, event | category | flops | bytes accessed | tf_op | source)
XLA Modules:
  0.0 132.0 jit_solution(8163373115647423038)
XLA Ops:
  0.6 126.4 %shard_map.67 = (bf16[128,384]{1,0:T(8,128)(2,1)}, bf16[384,1536]{1,0:T(8,128)(2,1)}, bf16[1536,384]{1,0:T(8,128)(2,1)}) custom-call(bf16[128,384]{1,0:T(8,128)(2,1)} %lat.1, bf16[384,1536]{1,0:T(8,128)(2,1)} %w_in.1, bf16[1536,384]{1,0:T(8,128)(2,1)} %w_out.1, bf16[128,384]{1,0:T(8,128)(2,1)} %cot.1), custom_call_target="tpu_custom_call" | custom-call | flops 12000000000 | bytes 5000000 | tf_op jit(solution)/shard_map/pallas_call | solution.py:352
  127.0 1.5 %copy.10 = bf16[128,384]{1,0:T(8,128)(2,1)} copy(bf16[128,384]{1,0:T(8,128)(2,1)} %get-tuple-element.6) | data formatting | bytes 196608
  128.6 0.0 copy-start
  128.6 2.5 %copy.11 = bf16[384,1536]{1,0:T(8,128)(2,1)} copy(bf16[384,1536]{1,0:T(8,128)(2,1)} %get-tuple-element.7) | data formatting | bytes 2359296
  131.0 0.0 copy-done
  131.0 1.0 copy.12
Async XLA Ops:
  128.6 2.5 %copy-start = (bf16[1536,384]{1,0:T(8,128)(2,1)S(1)}, bf16[1536,384]{1,0:T(8,128)(2,1)}, u32[]{:S(2)}) copy-start(bf16[1536,384]{1,0:T(8,128)(2,1)} %get-tuple-element.8) | copy-start | bytes 3538948

commit v3 on v2

v3 whole, which is shorter than its diff:
```python
import jax
import jax.numpy as jnp
from jax import lax
from jax.experimental import pallas as pl
from jax.experimental.pallas import tpu as pltpu
from jax.sharding import PartitionSpec as P

MESH = pl.DeviceIdType.MESH
BF = jnp.bfloat16
F32 = jnp.float32

TOK, FEAT, HID = 128, 384, 1536
ROWS, WIDE = 256, 768
CH = 8
RF0, RF, RB0, RB = 0, 1, 11, 1
GF0, GF, GB0, GB1 = 8, 1, 23, 1
LF, LB, MF, MB = 2, 3, 2, 3
COT = 6, 8
TICKS = GB0 + 7 * GB1 + 2 * MB + 1
BAND, PART, BIT = 128, 32, 16
PIECE, HALF = 64, 32

NN = (((1,), (0,)), ((), ()))
NT = (((1,), (1,)), ((), ()))
TN = (((0,), (0,)), ((), ()))


def dot(a, b, dims):
    return lax.dot_general(a, b, dims, preferred_element_type=F32)


def kernel(
    lat, w_in, w_out, cot,
    mixed, g_in, g_out,
    X, WI, WO, PT, FAR, CMB, RX, YB, YS, YR, SL, A, MO, MS, MR, MT, MIX, SIDE, OUT, GW, GB,
    s_loc, s_w, s_ws, s_x, s_xs, s_c, s_cs, s_far, s_rx, s_yr, s_ya, s_ag, s_fw,
    s_snd, s_mr, s_ms, s_mix, s_mixs, s_side, s_g, s_gs, s_gl,
):
    row, col = lax.axis_index("row"), lax.axis_index("col")
    x, yh, core = row // 4, (row // 2) % 2, row % 2
    yl, z = col // 8, col % 8

    def dev(x=x, yh=yh, core=core, yl=yl, z=z):
        return ((x * 2 + yh) * 2 + core, yl * 8 + z)

    right, left, across = (x + 1) % 4, (x + 3) % 4, (x + 2) % 4
    east, west = dev(x=right), dev(x=left)
    twin = dev(core=1 - core)
    pair = dev(yh=1 - yh)
    beside = dev(yl=1 - yl)
    up, down = dev(z=(z + 1) % 8), dev(z=(z + 7) % 8)

    barrier = pltpu.get_barrier_semaphore()
    peers = [east, west, twin, pair, beside] + [dev(z=(z + i) % 8) for i in range(1, 8)]
    for peer in peers:
        pl.semaphore_signal(barrier, inc=1, device_id=peer, device_id_type=MESH)

    def send(src, dst, send_sem, recv_sem, to):
        pltpu.make_async_remote_copy(
            src_ref=src, dst_ref=dst, send_sem=send_sem, recv_sem=recv_sem,
            device_id=to, device_id_type=MESH,
        ).start()

    def wait(ref, sem):
        pltpu.make_async_copy(ref, ref, sem).wait()

    def ds(start, size):
        return pl.ds(pl.multiple_of(start, size), size)

    mine = ds(core * WIDE, WIDE)
    other = ds((1 - core) * WIDE, WIDE)
    own, far = pl.ds(0, FEAT), pl.ds(FEAT, FEAT)
    s0, s1 = pl.ds(0, TOK), pl.ds(TOK, TOK)

    local = [
        pltpu.make_async_copy(lat, X.at[0, s0, own], s_loc.at[0]),
        pltpu.make_async_copy(w_in.at[:, mine], WI.at[own], s_loc.at[1]),
        pltpu.make_async_copy(w_out.at[mine], WO.at[:, own], s_loc.at[2]),
        pltpu.make_async_copy(cot, X.at[8, s0, own], s_loc.at[3]),
    ]
    for c in local:
        c.start()

    pl.semaphore_wait(barrier, len(peers))

    def first(src, j):
        send(src, X.at[j, s0, far], s_cs.at[j], s_c.at[j], twin)
        send(src, X.at[j, s1, own], s_xs.at[j], s_x.at[j], beside)
        send(src, X.at[j + 1, s0, own], s_xs.at[j], s_x.at[j + 1], up)
        send(src, X.at[j + 1, s1, own], s_xs.at[j], s_x.at[j + 1], down)

    def second(j):
        block = X.at[j, s1, own]
        wait(block, s_x.at[j])
        send(block, X.at[j + 2, s0, own], s_xs.at[j], s_x.at[j + 2], up)
        send(block, X.at[j + 2, s1, own], s_xs.at[j], s_x.at[j + 2], down)
        send(block, X.at[j, s1, far], s_cs.at[j], s_c.at[j], twin)

    first(lat, 0)
    send(w_in.at[:, other], WI.at[far], s_ws.at[0], s_w.at[0], twin)
    send(w_out.at[other], WO.at[:, far], s_ws.at[1], s_w.at[1], twin)
    second(0)
    for c in local:
        c.wait()
    wait(WI.at[own], s_w.at[0])
    wait(WO.at[:, own], s_w.at[1])

    def gather(j, fwd):
        k = j % CH
        whole = X.at[j, :, own]
        wait(whole, s_x.at[j])
        send(whole, X.at[j, :, far], s_cs.at[j], s_c.at[j], twin)
        low, high = X.at[j, s0, own], X.at[j, s1, own]

        @pl.when(k <= 5)
        def _():
            send(low, X.at[j + 2, s0, own], s_xs.at[j], s_x.at[j + 2], up)

        @pl.when(k <= 4)
        def _():
            send(high, X.at[j + 2, s1, own], s_xs.at[j], s_x.at[j + 2], down)

        @pl.when(k == 6)
        def _():
            send(high, X.at[j + 1, s1, own], s_xs.at[j], s_x.at[j + 1], down)

    def x_first(j):
        return (j % 2 == 0) | (j % CH == CH - 1)

    def y_first(j):
        return (j % 2 == 1) & (j % CH != CH - 1)

    def either(f, g):
        def chosen(j, fwd):
            pl.when(x_first(j))(lambda: f(j, fwd))
            pl.when(y_first(j))(lambda: g(j, fwd))

        return chosen

    def pointwise(j, fwd, h, here, rows):
        if fwd:
            cdf = 0.5 * (1.0 + lax.erf(h * 0.7071067811865476))
            pdf = jnp.exp(-0.5 * h * h) * 0.3989422804014327
            A[j, here, :] = (h * cdf).astype(BF)
            SL[j, pl.ds(0, rows), :] = cdf + h * pdf
        else:
            A[j, here, :] = (h * SL[j - CH, pl.ds(0, rows), :]).astype(BF)

    def part(j, fwd):
        wait(X.at[j, :, own], s_c.at[j])

        PT[j] = (dot(X[j], WI[...], NN) if fwd else dot(X[j], WO[...], NT)).astype(BF)
        ss = s_snd.at[j]

        @pl.when(x_first(j))
        def _():
            send(PT.at[j, ds(across * PIECE, HALF)], FAR.at[j, 0], ss, s_far.at[j], east)
            send(PT.at[j, ds(across * PIECE + HALF, HALF)], FAR.at[j, 1], ss, s_far.at[j], west)
            send(PT.at[j, ds(right * PIECE + HALF, HALF)], RX.at[j, 0, pl.ds(HALF, HALF)], ss, s_rx.at[j], east)
            send(PT.at[j, ds(left * PIECE, HALF)], RX.at[j, 1, pl.ds(0, HALF)], ss, s_rx.at[j], west)

        @pl.when(y_first(j))
        def _():
            send(PT.at[j, ds((1 - yh) * BAND, BAND)], YB.at[j // 2], ss, s_yr.at[j], pair)

    def combine(j, fwd):
        wait(FAR.at[j], s_far.at[j])
        ss = s_snd.at[j]
        a = PT[j, ds(right * PIECE, HALF), :].astype(F32) + FAR[j, 0].astype(F32)
        CMB[j, 0] = a.astype(BF)
        b = PT[j, ds(left * PIECE + HALF, HALF), :].astype(F32) + FAR[j, 1].astype(F32)
        CMB[j, 1] = b.astype(BF)
        send(CMB.at[j, 0], RX.at[j, 0, pl.ds(0, HALF)], ss, s_rx.at[j], east)
        send(CMB.at[j, 1], RX.at[j, 1, pl.ds(HALF, HALF)], ss, s_rx.at[j], west)

    def total(j, fwd):
        wait(RX.at[j], s_rx.at[j])
        t = PT[j, ds(x * PIECE, PIECE), :].astype(F32)
        YS[j] = (t + RX[j, 0].astype(F32) + RX[j, 1].astype(F32)).astype(BF)
        send(YS.at[j], YR.at[j], s_snd.at[j], s_yr.at[j], pair)

    def spread(j, fwd):
        wait(YR.at[j], s_yr.at[j])
        here = ds(x * PIECE, PIECE)
        pointwise(j, fwd, YS[j].astype(F32) + YR[j].astype(F32), here, PIECE)
        block = A.at[j, here]
        send(block, block, s_snd.at[j], s_ag.at[j], east)
        send(block, block, s_snd.at[j], s_ag.at[j], west)

    def onward(j, fwd):
        wait(RX.at[j], s_ag.at[j])
        a = A.at[j, ds(left * PIECE, HALF)]
        b = A.at[j, ds(right * PIECE + HALF, HALF)]
        send(a, a, s_snd.at[j], s_fw.at[j], east)
        send(b, b, s_snd.at[j], s_fw.at[j], west)

    band = yh * BAND

    def fold(j, fwd):
        wait(YB.at[j // 2], s_yr.at[j])
        rows = ds(band, BAND)
        PT[j, rows, :] = (PT[j, rows, :].astype(F32) + YB[j // 2].astype(F32)).astype(BF)
        ss = s_snd.at[j]
        lo, hi = pl.ds(0, BIT), pl.ds(BIT, BIT)
        send(PT.at[j, ds(band + across * PART, BIT)], FAR.at[j, 0, lo], ss, s_far.at[j], east)
        send(PT.at[j, ds(band + across * PART + BIT, BIT)], FAR.at[j, 1, lo], ss, s_far.at[j], west)
        send(PT.at[j, ds(band + right * PART + BIT, BIT)], RX.at[j, 0, hi], ss, s_rx.at[j], east)
        send(PT.at[j, ds(band + left * PART, BIT)], RX.at[j, 1, lo], ss, s_rx.at[j], west)

    def combine_y(j, fwd):
        wait(FAR.at[j, 0], s_far.at[j])
        ss = s_snd.at[j]
        lo, hi = pl.ds(0, BIT), pl.ds(BIT, BIT)
        a = PT[j, ds(band + right * PART, BIT), :].astype(F32) + FAR[j, 0, lo, :].astype(F32)
        CMB[j, 0, lo, :] = a.astype(BF)
        b = PT[j, ds(band + left * PART + BIT, BIT), :].astype(F32) + FAR[j, 1, lo, :].astype(F32)
        CMB[j, 1, lo, :] = b.astype(BF)
        send(CMB.at[j, 0, lo], RX.at[j, 0, lo], ss, s_rx.at[j], east)
        send(CMB.at[j, 1, lo], RX.at[j, 1, hi], ss, s_rx.at[j], west)

    def point_y(j, fwd):
        wait(RX.at[j, 0], s_rx.at[j])
        here = ds(band + x * PART, PART)
        h = PT[j, here, :].astype(F32) + RX[j, 0, pl.ds(0, PART), :].astype(F32)
        pointwise(j, fwd, h + RX[j, 1, pl.ds(0, PART), :].astype(F32), here, PART)
        block = A.at[j, here]
        send(block, block, s_snd.at[j], s_ag.at[j], east)
        send(block, block, s_snd.at[j], s_ag.at[j], west)

    def onward_y(j, fwd):
        wait(RX.at[j, 0], s_ag.at[j])
        a = A.at[j, ds(band + left * PART, BIT)]
        b = A.at[j, ds(band + right * PART + BIT, BIT)]
        send(a, a, s_snd.at[j], s_fw.at[j], east)
        send(b, b, s_snd.at[j], s_fw.at[j], west)

    def spread_y(j, fwd):
        wait(YR.at[j, pl.ds(0, PART)], s_fw.at[j])
        block = A.at[j, ds(band, BAND)]
        send(block, block, s_snd.at[j], s_ya.at[j], pair)

    def use(j, fwd):
        either(
            lambda j, fwd: wait(FAR.at[j], s_fw.at[j]),
            lambda j, fwd: wait(RX.at[j], s_ya.at[j]),
        )(j, fwd)
        if not fwd:
            GW[1] = GW[1] + dot(X[j - CH], A[j], TN)
            return

        m = dot(A[j], WO[...], NN)
        MS[j] = m[:, FEAT:].astype(BF)
        send(MS.at[j], MR.at[j], s_ms.at[j], s_mr.at[j], twin)
        MO[j] = m[:, :FEAT]
        GW[0] = GW[0] + dot(A[j], X[j + CH], TN)

        @pl.when(j == CH - 1)
        def _():
            GB[0] = GW[0].astype(BF)
            pltpu.make_async_copy(GB.at[0, :, own], g_out.at[mine], s_gl.at[0]).start()
            send(GB.at[0, :, far], g_out.at[mine], s_gs.at[0], s_g.at[0], twin)

    def mix(j, fwd):
        wait(MS.at[j], s_mr.at[j])
        MT[j] = (MO[j] + MR[j].astype(F32)).astype(BF)
        m = (j + 1) // 2
        below, above = (z + 8 - m) % 8, (z + m) % 8
        low, high = MT.at[j, s0], MT.at[j, s1]
        sems = s_mixs.at[j], s_mix

        @pl.when((j > 0) & (j < CH - 1))
        def _():
            line = (j + 1) % 2
            send(low, MIX.at[line, j - line - 1], *sems, dev(z=below))
            send(high, MIX.at[line, j - line], *sems, dev(z=above))

        @pl.when(j == CH - 1)
        def _():
            send(low, MIX.at[0, 6], *sems, dev(z=above))
            send(high, MIX.at[1, 6], *sems, dev(z=above))

    GW[...] = jnp.zeros_like(GW)

    def stage(f, t, fwd, start, step):
        t = t - start
        due = (t >= 0) & (t < 8 * step) & (t % step == 0)
        pl.when(due)(lambda: f(t // step + (0 if fwd else CH), fwd))

    def reduce_stage(f, t, lags):
        stage(f, t - lags * LF, True, RF0, RF)
        stage(f, t - lags * LB, False, RB0, RB)

    def spread_stage(f, t, lags):
        stage(f, t - lags * MF, True, GF0, GF)
        stage(f, t - lags * MB, False, GB0, GB1)

    def idle(j, fwd):
        pass

    def next_gather(j, fwd):
        pl.when(j % CH != CH - 1)(lambda: gather(j + 1, fwd))

    def line_total(line):
        t = MT[0, pl.ds(line * TOK, TOK), :].astype(F32)
        for k in range(7):
            t = t + MIX[line, k].astype(F32)
        return t

    def finish_other():
        wait(MIX, s_mix)
        SIDE[0] = line_total(1).astype(BF)
        send(SIDE.at[0], SIDE.at[1], s_side.at[0], s_side.at[1], beside)

    def finish_own():
        t = line_total(0)
        wait(SIDE.at[1], s_side.at[1])
        OUT[...] = (t + SIDE[1].astype(F32)).astype(BF)
        pltpu.make_async_copy(OUT, mixed, s_gl.at[2]).start()

    def step(t, carry):
        reduce_stage(next_gather, t, 0)
        reduce_stage(part, t, 0)
        spread_stage(either(onward, spread_y), t, 1)
        spread_stage(either(spread, onward_y), t, 0)
        reduce_stage(either(idle, point_y), t, 3)
        reduce_stage(either(total, combine_y), t, 2)
        reduce_stage(either(combine, fold), t, 1)
        stage(mix, t - 2 * MF - 1, True, GF0, GF)
        spread_stage(use, t, 2)

        pl.when(t == TICKS - 3)(finish_other)

        @pl.when(t == COT[0])
        def _():
            first(cot, CH)

        @pl.when(t == COT[1])
        def _():
            second(CH)

        return carry

    lax.fori_loop(0, TICKS, step, 0)

    GB[1] = GW[1].astype(BF)
    send(GB.at[1, far], g_in.at[:, mine], s_gs.at[1], s_g.at[1], twin)
    last = pltpu.make_async_copy(GB.at[1, own], g_in.at[:, mine], s_gl.at[1])
    last.start()

    finish_own()

    wait(WI.at[own], s_ws.at[0])
    wait(WO.at[:, own], s_ws.at[1])

    def drain(j, carry):
        k = j % CH
        wait(A.at[pl.ds(0, 7), pl.ds(0, PIECE)], s_snd.at[j])
        wait(X.at[j, :, own], s_cs.at[j])

        @pl.when(k == 0)
        def _():
            wait(MIX.at[0, pl.ds(0, 5)], s_xs.at[j])

        @pl.when((k > 0) & (k <= 4))
        def _():
            wait(X.at[j, :, own], s_xs.at[j])

        @pl.when((k == 5) | (k == 6))
        def _():
            wait(X.at[j, s0, own], s_xs.at[j])

        @pl.when(j < CH)
        def _():
            wait(MS.at[j], s_ms.at[j])

        @pl.when((j < CH) & (j > 0))
        def _():
            wait(MT.at[j], s_mixs.at[j])

        return carry

    lax.fori_loop(0, 16, drain, 0)
    for i, (ref, half) in enumerate(((g_out.at[mine], GB.at[0, :, own]), (g_in.at[:, mine], GB.at[1, own]))):
        wait(half, s_gs.at[i])
        wait(half, s_g.at[i])
        wait(half, s_gl.at[i])
    wait(SIDE.at[0], s_side.at[0])
    wait(OUT, s_gl.at[2])


def per_device(latents, w_in, w_out, cotangent):
    anyspec = pl.BlockSpec(memory_space=pl.ANY)
    V, D = pltpu.VMEM, pltpu.SemaphoreType.DMA
    return pl.pallas_call(
        kernel,
        out_shape=(V((TOK, FEAT), BF), V((FEAT, HID), BF), V((HID, FEAT), BF)),
        in_specs=[anyspec] * 4,
        out_specs=[anyspec] * 3,
        scratch_shapes=[
            V((16, ROWS, WIDE), BF),
            V((WIDE, WIDE), BF),
            V((WIDE, WIDE), BF),
            V((16, ROWS, WIDE), BF),
            V((16, 2, HALF, WIDE), BF),
            V((16, 2, HALF, WIDE), BF),
            V((16, 2, PIECE, WIDE), BF),
            V((CH, BAND, WIDE), BF),
            V((16, PIECE, WIDE), BF),
            V((16, PIECE, WIDE), BF),
            V((CH, PIECE, WIDE), F32),
            V((16, ROWS, WIDE), BF),
            V((CH, ROWS, FEAT), F32),
            V((CH, ROWS, FEAT), BF),
            V((CH, ROWS, FEAT), BF),
            V((CH, ROWS, FEAT), BF),
            V((2, 7, TOK, FEAT), BF),
            V((2, TOK, FEAT), BF),
            V((TOK, FEAT), BF),
            V((2, WIDE, WIDE), F32),
            V((2, WIDE, WIDE), BF),
            D((4,)),
            D((2,)),
            D((2,)),
            D((16,)),
            D((16,)),
            D((16,)),
            D((16,)),
            D((16,)),
            D((16,)),
            D((16,)),
            D((16,)),
            D((16,)),
            D((16,)),
            D((16,)),
            D((CH,)),
            D((CH,)),
            D,
            D((CH,)),
            D((2,)),
            D((2,)),
            D((2,)),
            D((3,)),
        ],
        compiler_params=pltpu.CompilerParams(
            collective_id=0, has_side_effects=True, vmem_limit_bytes=58 * 1024 * 1024
        ),
        cost_estimate=pl.CostEstimate(
            flops=12 * 10**9, bytes_accessed=5 * 10**6, transcendentals=10**6
        ),
    )(latents, w_in, w_out, cotangent)


def solution(mesh):
    placed = (P("col", "row"), P("row", "col"), P("col", "row"), P("col", "row"))
    return jax.shard_map(
        per_device,
        mesh=mesh,
        in_specs=placed,
        out_specs=(P("col", "row"), P("row", "col"), P("col", "row")),
        check_vma=False,
    )
```

time: 132 us -> 117 us (0.89)
  Pallas kernels: 126 us -> 113 us
  local copies, waits for them, and re-layouts: 5.02 us -> 2.67 us
    pallas_call x1, Pallas kernels: 126 us -> 113 us  [per_device(): pl.pallas_call(kernel, out_shape=(V((TOK, FEAT), BF), V((FEAT, HID), BF),...]
    unnamed x5 -> x3, local copies, waits for them, and re-layouts: 5.02 us -> 2.67 us
where the time goes in v3:
time: 117 us
  Pallas kernels  113 us (97%)
  local copies, waits for them, and re-layouts  2.67 us (2%)
    pallas_call x1, Pallas kernels, per_device(): pl.pallas_call(kernel, out_shape=(V((TOK, FEAT), BF), V((FEAT, HID), BF),...  113 us
    unnamed x3, local copies, waits for them, and re-layouts  2.67 us

profile of v3, /device:TPU:1, one launch (start us, length us, event | category | flops | bytes accessed | tf_op | source)
XLA Modules:
  0.0 116.7 jit_solution(6871651014210449239)
XLA Ops:
  0.6 113.4 %shard_map.67 = (bf16[128,384]{1,0:T(8,128)(2,1)S(1)}, bf16[384,1536]{1,0:T(8,128)(2,1)S(1)}, bf16[1536,384]{1,0:T(8,128)(2,1)S(1)}) custom-call(bf16[128,384]{1,0:T(8,128)(2,1)} %lat.1, bf16[384,1536]{1,0:T(8,128)(2,1)} %w_in.1, bf16[1536,384]{1,0:T(8,128)(2,1)} %w_out.1, bf16[128,384]{1,0:T(8,128)(2,1)} %cot.1), custom_call_target="tpu_custom_call" | custom-call | flops 12000000000 | bytes 5000000 | tf_op jit(solution)/shard_map/pallas_call | solution.py:394
  114.1 0.6 copy.10
  114.7 1.0 copy.11
  115.7 1.0 copy.12

commit v4 on v3

--- a/solution.py
+++ b/solution.py
@@ -14,9 +14,11 @@
 CH = 8
 RF0, RF, RB0, RB = 0, 1, 11, 1
 GF0, GF, GB0, GB1 = 8, 1, 23, 1
-LF, LB, MF, MB = 2, 3, 2, 3
+FX, FY = (2, 4, 6, 2), (2, 4, 6, 2)
+BX, BY = (3, 6, 9, 3), (3, 6, 9, 3)
+UF, UB = 4, 6
 COT = 6, 8
-TICKS = GB0 + 7 * GB1 + 2 * MB + 1
+TICKS = GB0 + 7 * GB1 + UB + 1
 BAND, PART, BIT = 128, 32, 16
 PIECE, HALF = 64, 32
 
@@ -81,25 +83,34 @@
     for c in local:
         c.start()
 
+    GW[...] = jnp.zeros_like(GW)
     pl.semaphore_wait(barrier, len(peers))
 
-    def first(src, j):
+    def pieces(fwd):
+        size = TOK // 2 if fwd else TOK
+        return [(q, q * size, size) for q in range(TOK // size)]
+
+    def first(src, j, fwd):
+        for q, at, size in pieces(fwd):
+            rows, low, high = src.at[pl.ds(at, size)], pl.ds(at, size), pl.ds(TOK + at, size)
+            send(rows, X.at[j, high, own], s_xs.at[j], s_x.at[j, q], beside)
+            send(rows, X.at[j + 1, low, own], s_xs.at[j], s_x.at[j + 1, q], up)
+            send(rows, X.at[j + 1, high, own], s_xs.at[j], s_x.at[j + 1, q], down)
         send(src, X.at[j, s0, far], s_cs.at[j], s_c.at[j], twin)
-        send(src, X.at[j, s1, own], s_xs.at[j], s_x.at[j], beside)
-        send(src, X.at[j + 1, s0, own], s_xs.at[j], s_x.at[j + 1], up)
-        send(src, X.at[j + 1, s1, own], s_xs.at[j], s_x.at[j + 1], down)
-
-    def second(j):
-        block = X.at[j, s1, own]
-        wait(block, s_x.at[j])
-        send(block, X.at[j + 2, s0, own], s_xs.at[j], s_x.at[j + 2], up)
-        send(block, X.at[j + 2, s1, own], s_xs.at[j], s_x.at[j + 2], down)
-        send(block, X.at[j, s1, far], s_cs.at[j], s_c.at[j], twin)
-
-    first(lat, 0)
+
+    def second(j, fwd):
+        for q, at, size in pieces(fwd):
+            low, high = pl.ds(at, size), pl.ds(TOK + at, size)
+            block = X.at[j, high, own]
+            wait(block, s_x.at[j, q])
+            send(block, X.at[j + 2, low, own], s_xs.at[j], s_x.at[j + 2, q], up)
+            send(block, X.at[j + 2, high, own], s_xs.at[j], s_x.at[j + 2, q], down)
+        send(X.at[j, s1, own], X.at[j, s1, far], s_cs.at[j], s_c.at[j], twin)
+
+    first(lat, 0, True)
     send(w_in.at[:, other], WI.at[far], s_ws.at[0], s_w.at[0], twin)
     send(w_out.at[other], WO.at[:, far], s_ws.at[1], s_w.at[1], twin)
-    second(0)
+    second(0, True)
     for c in local:
         c.wait()
     wait(WI.at[own], s_w.at[0])
@@ -107,22 +118,25 @@
 
     def gather(j, fwd):
         k = j % CH
+        for q, at, size in pieces(fwd):
+            wait(X.at[j, pl.ds(0, 2 * size), own], s_x.at[j, q])
+            s_low, s_high = pl.ds(at, size), pl.ds(TOK + at, size)
+            low, high = X.at[j, s_low, own], X.at[j, s_high, own]
+
+            @pl.when(k <= 5)
+            def _():
+                send(low, X.at[j + 2, s_low, own], s_xs.at[j], s_x.at[j + 2, q], up)
+
+            @pl.when(k <= 4)
+            def _():
+                send(high, X.at[j + 2, s_high, own], s_xs.at[j], s_x.at[j + 2, q], down)
+
+            @pl.when(k == 6)
+            def _():
+                send(high, X.at[j + 1, s_high, own], s_xs.at[j], s_x.at[j + 1, q], down)
+
         whole = X.at[j, :, own]
-        wait(whole, s_x.at[j])
         send(whole, X.at[j, :, far], s_cs.at[j], s_c.at[j], twin)
-        low, high = X.at[j, s0, own], X.at[j, s1, own]
-
-        @pl.when(k <= 5)
-        def _():
-            send(low, X.at[j + 2, s0, own], s_xs.at[j], s_x.at[j + 2], up)
-
-        @pl.when(k <= 4)
-        def _():
-            send(high, X.at[j + 2, s1, own], s_xs.at[j], s_x.at[j + 2], down)
-
-        @pl.when(k == 6)
-        def _():
-            send(high, X.at[j + 1, s1, own], s_xs.at[j], s_x.at[j + 1], down)
 
     def x_first(j):
         return (j % 2 == 0) | (j % CH == CH - 1)
@@ -130,12 +144,11 @@
     def y_first(j):
         return (j % 2 == 1) & (j % CH != CH - 1)
 
-    def either(f, g):
-        def chosen(j, fwd):
-            pl.when(x_first(j))(lambda: f(j, fwd))
-            pl.when(y_first(j))(lambda: g(j, fwd))
-
-        return chosen
+    def when_x(f):
+        return lambda j, fwd: pl.when(x_first(j))(lambda: f(j, fwd))
+
+    def when_y(f):
+        return lambda j, fwd: pl.when(y_first(j))(lambda: f(j, fwd))
 
     def pointwise(j, fwd, h, here, rows):
         if fwd:
@@ -240,12 +253,13 @@
         send(block, block, s_snd.at[j], s_ya.at[j], pair)
 
     def use(j, fwd):
-        either(
-            lambda j, fwd: wait(FAR.at[j], s_fw.at[j]),
-            lambda j, fwd: wait(RX.at[j], s_ya.at[j]),
-        )(j, fwd)
+        pl.when(x_first(j))(lambda: wait(FAR.at[j], s_fw.at[j]))
+        pl.when(y_first(j))(lambda: wait(RX.at[j], s_ya.at[j]))
         if not fwd:
-            GW[1] = GW[1] + dot(X[j - CH], A[j], TN)
+            @pl.when(j < 15)
+            def _():
+                GW[1] = GW[1] + dot(X[j - CH], A[j], TN)
+
             return
 
         m = dot(A[j], WO[...], NN)
@@ -279,23 +293,42 @@
             send(low, MIX.at[0, 6], *sems, dev(z=above))
             send(high, MIX.at[1, 6], *sems, dev(z=above))
 
-    GW[...] = jnp.zeros_like(GW)
-
     def stage(f, t, fwd, start, step):
         t = t - start
         due = (t >= 0) & (t < 8 * step) & (t % step == 0)
         pl.when(due)(lambda: f(t // step + (0 if fwd else CH), fwd))
 
-    def reduce_stage(f, t, lags):
-        stage(f, t - lags * LF, True, RF0, RF)
-        stage(f, t - lags * LB, False, RB0, RB)
-
-    def spread_stage(f, t, lags):
-        stage(f, t - lags * MF, True, GF0, GF)
-        stage(f, t - lags * MB, False, GB0, GB1)
-
-    def idle(j, fwd):
-        pass
+    def reduce_stage(f, t, lags=(0, 0)):
+        stage(f, t - lags[0], True, RF0, RF)
+        stage(f, t - lags[1], False, RB0, RB)
+
+    def spread_stage(f, t, lags=(0, 0)):
+        stage(f, t - lags[0], True, GF0, GF)
+        stage(f, t - lags[1], False, GB0, GB1)
+
+    def drain(j, fwd):
+        k = j % CH
+        wait(A.at[pl.ds(0, 7), pl.ds(0, PIECE)], s_snd.at[j])
+        wait(X.at[j, :, own], s_cs.at[j])
+
+        @pl.when(k == 0)
+        def _():
+            wait(MIX.at[0, pl.ds(0, 5)], s_xs.at[j])
+
+        @pl.when((k > 0) & (k <= 4))
+        def _():
+            wait(X.at[j, :, own], s_xs.at[j])
+
+        @pl.when((k == 5) | (k == 6))
+        def _():
+            wait(X.at[j, s0, own], s_xs.at[j])
+
+        if not fwd:
+            wait(MS.at[k], s_ms.at[k])
+
+            @pl.when(k > 0)
+            def _():
+                wait(MT.at[k], s_mixs.at[k])
 
     def next_gather(j, fwd):
         pl.when(j % CH != CH - 1)(lambda: gather(j + 1, fwd))
@@ -318,32 +351,38 @@
         pltpu.make_async_copy(OUT, mixed, s_gl.at[2]).start()
 
     def step(t, carry):
-        reduce_stage(next_gather, t, 0)
-        reduce_stage(part, t, 0)
-        spread_stage(either(onward, spread_y), t, 1)
-        spread_stage(either(spread, onward_y), t, 0)
-        reduce_stage(either(idle, point_y), t, 3)
-        reduce_stage(either(total, combine_y), t, 2)
-        reduce_stage(either(combine, fold), t, 1)
-        stage(mix, t - 2 * MF - 1, True, GF0, GF)
-        spread_stage(use, t, 2)
+        reduce_stage(part, t)
+        reduce_stage(next_gather, t)
+        spread_stage(when_x(onward), t, (FX[3], BX[3]))
+        spread_stage(when_y(spread_y), t, (FY[3], BY[3]))
+        spread_stage(when_x(spread), t)
+        spread_stage(when_y(onward_y), t)
+        reduce_stage(when_y(point_y), t, (FY[2], BY[2]))
+        reduce_stage(when_x(total), t, (FX[1], BX[1]))
+        reduce_stage(when_y(combine_y), t, (FY[1], BY[1]))
+        reduce_stage(when_x(combine), t, (FX[0], BX[0]))
+        reduce_stage(when_y(fold), t, (FY[0], BY[0]))
+        stage(mix, t - UF - 1, True, GF0, GF)
+        spread_stage(use, t, (UF, UB))
+        spread_stage(drain, t, (UF, UB))
 
         pl.when(t == TICKS - 3)(finish_other)
 
         @pl.when(t == COT[0])
         def _():
-            first(cot, CH)
+            first(cot, CH, False)
 
         @pl.when(t == COT[1])
         def _():
-            second(CH)
+            second(CH, False)
 
         return carry
 
     lax.fori_loop(0, TICKS, step, 0)
 
-    GB[1] = GW[1].astype(BF)
+    GB[1, far, :] = (GW[1, far, :] + dot(X[CH - 1, :, far], A[15], TN)).astype(BF)
     send(GB.at[1, far], g_in.at[:, mine], s_gs.at[1], s_g.at[1], twin)
+    GB[1, own, :] = (GW[1, own, :] + dot(X[CH - 1, :, own], A[15], TN)).astype(BF)
     last = pltpu.make_async_copy(GB.at[1, own], g_in.at[:, mine], s_gl.at[1])
     last.start()
 
@@ -352,34 +391,6 @@
     wait(WI.at[own], s_ws.at[0])
     wait(WO.at[:, own], s_ws.at[1])
 
-    def drain(j, carry):
-        k = j % CH
-        wait(A.at[pl.ds(0, 7), pl.ds(0, PIECE)], s_snd.at[j])
-        wait(X.at[j, :, own], s_cs.at[j])
-
-        @pl.when(k == 0)
-        def _():
-            wait(MIX.at[0, pl.ds(0, 5)], s_xs.at[j])
-
-        @pl.when((k > 0) & (k <= 4))
-        def _():
-            wait(X.at[j, :, own], s_xs.at[j])
-
-        @pl.when((k == 5) | (k == 6))
-        def _():
-            wait(X.at[j, s0, own], s_xs.at[j])
-
-        @pl.when(j < CH)
-        def _():
-            wait(MS.at[j], s_ms.at[j])
-
-        @pl.when((j < CH) & (j > 0))
-        def _():
-            wait(MT.at[j], s_mixs.at[j])
-
-        return carry
-
-    lax.fori_loop(0, 16, drain, 0)
     for i, (ref, half) in enumerate(((g_out.at[mine], GB.at[0, :, own]), (g_in.at[:, mine], GB.at[1, own]))):
         wait(half, s_gs.at[i])
         wait(half, s_g.at[i])
@@ -421,7 +432,7 @@
             D((4,)),
             D((2,)),
             D((2,)),
-            D((16,)),
+            D((16, 2)),
             D((16,)),
             D((16,)),
             D((16,)),

time: 117 us -> 114 us (0.974)
  Pallas kernels: 113 us -> 111 us
    pallas_call x1, Pallas kernels: 113 us -> 111 us  [per_device(): pl.pallas_call(kernel, out_shape=(V((TOK, FEAT), BF), V((FEAT, HID), BF),...]
where the time goes in v4:
time: 114 us
  Pallas kernels  111 us (97%)
  local copies, waits for them, and re-layouts  2.67 us (2%)
    pallas_call x1, Pallas kernels, per_device(): pl.pallas_call(kernel, out_shape=(V((TOK, FEAT), BF), V((FEAT, HID), BF),...  111 us
    unnamed x3, local copies, waits for them, and re-layouts  2.67 us

profile of v4, /device:TPU:1, one launch (start us, length us, event | category | flops | bytes accessed | tf_op | source)
XLA Modules:
  0.0 114.2 jit_solution(903426899036930166)
XLA Ops:
  0.6 110.9 %shard_map.67 = (bf16[128,384]{1,0:T(8,128)(2,1)S(1)}, bf16[384,1536]{1,0:T(8,128)(2,1)S(1)}, bf16[1536,384]{1,0:T(8,128)(2,1)S(1)}) custom-call(bf16[128,384]{1,0:T(8,128)(2,1)} %lat.1, bf16[384,1536]{1,0:T(8,128)(2,1)} %w_in.1, bf16[1536,384]{1,0:T(8,128)(2,1)} %w_out.1, bf16[128,384]{1,0:T(8,128)(2,1)} %cot.1), custom_call_target="tpu_custom_call" | custom-call | flops 12000000000 | bytes 5000000 | tf_op jit(solution)/shard_map/pallas_call | solution.py:405
  111.6 0.6 copy.10
  112.2 1.0 copy.11
  113.2 1.0 copy.12

commit v5 on v4

--- a/solution.py
+++ b/solution.py
@@ -12,11 +12,11 @@
 TOK, FEAT, HID = 128, 384, 1536
 ROWS, WIDE = 256, 768
 CH = 8
-RF0, RF, RB0, RB = 0, 1, 11, 1
-GF0, GF, GB0, GB1 = 8, 1, 23, 1
+RF0, RF, RB0, RB = 0, 1, 10, 1
+GF0, GF, GB0, GB1 = 9, 1, 22, 1
 FX, FY = (2, 4, 6, 2), (2, 4, 6, 2)
-BX, BY = (3, 6, 9, 3), (3, 6, 9, 3)
-UF, UB = 4, 6
+BX, BY = (3, 6, 9, 4), (3, 6, 9, 3)
+UF, UB = 4, 7
 COT = 6, 8
 TICKS = GB0 + 7 * GB1 + UB + 1
 BAND, PART, BIT = 128, 32, 16

time: 114 us -> 113 us (level)
  Pallas kernels: 111 us -> 109 us
    pallas_call x1, Pallas kernels: 111 us -> 109 us  [per_device(): pl.pallas_call(kernel, out_shape=(V((TOK, FEAT), BF), V((FEAT, HID), BF),...]
where the time goes in v5:
time: 113 us
  Pallas kernels  109 us (96%)
  local copies, waits for them, and re-layouts  2.67 us (2%)
    pallas_call x1, Pallas kernels, per_device(): pl.pallas_call(kernel, out_shape=(V((TOK, FEAT), BF), V((FEAT, HID), BF),...  109 us
    unnamed x3, local copies, waits for them, and re-layouts  2.67 us

profile of v5, /device:TPU:1, one launch (start us, length us, event | category | flops | bytes accessed | tf_op | source)
XLA Modules:
  0.0 112.7 jit_solution(10112262271459837491)
XLA Ops:
  0.6 109.4 %shard_map.67 = (bf16[128,384]{1,0:T(8,128)(2,1)S(1)}, bf16[384,1536]{1,0:T(8,128)(2,1)S(1)}, bf16[1536,384]{1,0:T(8,128)(2,1)S(1)}) custom-call(bf16[128,384]{1,0:T(8,128)(2,1)} %lat.1, bf16[384,1536]{1,0:T(8,128)(2,1)} %w_in.1, bf16[1536,384]{1,0:T(8,128)(2,1)} %w_out.1, bf16[128,384]{1,0:T(8,128)(2,1)} %cot.1), custom_call_target="tpu_custom_call" | custom-call | flops 12000000000 | bytes 5000000 | tf_op jit(solution)/shard_map/pallas_call | solution.py:405
  110.1 0.6 copy.10
  110.7 1.0 copy.11
  111.7 1.0 copy.12

commit v6 on v5

--- a/solution.py
+++ b/solution.py
@@ -14,7 +14,7 @@
 CH = 8
 RF0, RF, RB0, RB = 0, 1, 10, 1
 GF0, GF, GB0, GB1 = 9, 1, 22, 1
-FX, FY = (2, 4, 6, 2), (2, 4, 6, 2)
+FX, FY = (2, 4, 6, 2), (3, 4, 6, 2)
 BX, BY = (3, 6, 9, 4), (3, 6, 9, 3)
 UF, UB = 4, 7
 COT = 6, 8

time: 113 us -> 115 us (1.018)
  Pallas kernels: 109 us -> 112 us
    pallas_call x1, Pallas kernels: 109 us -> 112 us  [per_device(): pl.pallas_call(kernel, out_shape=(V((TOK, FEAT), BF), V((FEAT, HID), BF),...]
where the time goes in v6:
time: 115 us
  Pallas kernels  112 us (97%)
  local copies, waits for them, and re-layouts  2.67 us (2%)
    pallas_call x1, Pallas kernels, per_device(): pl.pallas_call(kernel, out_shape=(V((TOK, FEAT), BF), V((FEAT, HID), BF),...  112 us
    unnamed x3, local copies, waits for them, and re-layouts  2.67 us

profile of v6, /device:TPU:1, one launch (start us, length us, event | category | flops | bytes accessed | tf_op | source)
XLA Modules:
  0.0 114.9 jit_solution(2464292005756396022)
XLA Ops:
  0.6 111.5 %shard_map.67 = (bf16[128,384]{1,0:T(8,128)(2,1)S(1)}, bf16[384,1536]{1,0:T(8,128)(2,1)S(1)}, bf16[1536,384]{1,0:T(8,128)(2,1)S(1)}) custom-call(bf16[128,384]{1,0:T(8,128)(2,1)} %lat.1, bf16[384,1536]{1,0:T(8,128)(2,1)} %w_in.1, bf16[1536,384]{1,0:T(8,128)(2,1)} %w_out.1, bf16[128,384]{1,0:T(8,128)(2,1)} %cot.1), custom_call_target="tpu_custom_call" | custom-call | flops 12000000000 | bytes 5000000 | tf_op jit(solution)/shard_map/pallas_call | solution.py:405
  112.2 0.6 copy.10
  112.8 1.0 copy.11
  113.8 1.0 copy.12
